TPU v7x, 32 devices: a whole 2x2x4 slice. The times are simulated.
32 devices in a mesh: grp: 2 (over x), doc: 16 (over z, y, core).
Axes of the slice: x: 2, y: 2, z: 4, core: 2. Of those that a mesh axis runs over, the one named last changes fastest.
Arguments:
- doc_grads: bfloat16 [16, 512, 32768], P('doc', 'grp'), parts along dimension 1, may hold values from -6 to 6
- query_grads: bfloat16 [16, 2048, 32768], P('doc', 'grp'), parts along dimension 1, may hold values from -180 to 180
Outputs:
- influence: float32 [8192, 1024], P(('grp', 'doc')), parts along dimension 0
There are 2 independent parts, one for each index of `grp`. A program takes and returns all parts, laid end to end along the dimension named above; each array names one. Nothing has to cross between parts.
All inputs are finite; a program needn't handle non-finite values.
Results may differ from a plain program's by a relative error of at most 0.0003.
Values may be sent and summed in bfloat16 or wider, within the bound.
A program may use at most 256 MiB of HBM per device.

v0:
```python
import jax
import jax.numpy as jnp
from jax import lax
from jax.sharding import PartitionSpec as P

epsilon = 1e-06


def from_partner(value, axis, stride):
    return lax.ppermute(value, axis, [(i, i ^ 1 << stride) for i in range(lax.axis_size(axis))])


def shifted(value, axis, steps):
    count = lax.axis_size(axis)
    pairs = [(source, (source + steps) % count) for source in range(count)]
    return lax.ppermute(value, axis, pairs)


def block_halving(block, index, levels):
    for level in reversed(range(levels)):
        half = block.shape[0] // 2
        bit = index >> level & 1
        keep = lax.dynamic_slice_in_dim(block, bit * half, half, 0)
        outgoing = lax.dynamic_slice_in_dim(block, (1 - bit) * half, half, 0)
        block = keep + from_partner(outgoing, "doc", level)
    return block


def on_device(doc_grads, query_grads):
    doc_tile = doc_grads[0]
    query_tile = query_grads[0]
    span = lax.axis_size("doc") // 4
    levels = span.bit_length() - 1
    index = lax.axis_index("doc")
    group = index // span
    contract = (((1,), (1,)), ((), ()))

    def partial_scores(tile):
        return lax.dot_general(query_tile, tile, contract, preferred_element_type=jnp.float32)

    tiles = [doc_tile]
    for step in range(3):
        tiles.append(shifted(tiles[-1], "doc", span))
    order = (group - jnp.arange(4, dtype=jnp.int32)) % 4
    summed = [block_halving(partial_scores(tile), index, levels) for tile in tiles]
    stacked = jnp.stack(summed, 1)
    placed = jnp.take(stacked, order, axis=1)
    scores = placed.reshape(placed.shape[0], placed.shape[1] * placed.shape[2])
    squares = lax.psum(jnp.sum(scores * scores, axis=0), "doc")
    inv_spread = lax.rsqrt(squares / (4 * query_tile.shape[0]) + epsilon)
    return scores * inv_spread[None, :]


def solution(mesh):
    placed = (P("doc", "grp", None), P("doc", "grp", None))
    return jax.shard_map(
        on_device, mesh=mesh, in_specs=placed, out_specs=P(("grp", "doc"), None), check_vma=False
    )
```

profile of v0, /device:TPU:0, one launch (start us, length us, event | category | flops | bytes accessed | tf_op | source)
XLA Modules:
  0.0 1172.5 jit_solution(906279781229463260)
XLA Ops:
  0.0 3.0 collective-permute-start.2
  3.0 362.5 %collective-permute-done.2 = bf16[256,32768]{1,0:T(8,128)(2,1)S(1)} collective-permute-done((bf16[256,32768]{1,0:T(8,128)(2,1)}, bf16[256,32768]{1,0:T(8,128)(2,1)S(1)}, u32[]{:S(2)}, u32[]{:S(2)}) %collective-permute-start.2) | collective-permute-done | bytes 16777248 | tf_op jit(solution)/shard_map/ppermute | solution.py:16
  365.5 5.7 copy-done
  371.2 363.3 %collective-permute-done.5 = bf16[256,32768]{1,0:T(8,128)(2,1)} collective-permute-done((bf16[256,32768]{1,0:T(8,128)(2,1)S(1)}, bf16[256,32768]{1,0:T(8,128)(2,1)}, u32[]{:S(2)}, u32[]{:S(2)}) %collective-permute-start.5) | collective-permute-done | bytes 16777248 | tf_op jit(solution)/shard_map/ppermute | solution.py:16
  734.5 29.7 %fusion.6 = f32[1024,256]{1,0:T(8,128)S(1)} fusion(bf16[1,1024,32768]{2,1,0:T(8,128)(2,1)} %param.3, bf16[1,256,32768]{2,1,0:T(8,128)(2,1)} %param.2), kind=kOutput, calls=%fused_computation.7 | convolution fusion | flops 17179869184 | bytes 84934656 | tf_op jit(solution)/shard_map/dot_general | solution.py:39
  764.2 1.3 collective-permute-start
  765.5 10.9 collective-permute-done
  776.8 1.4 collective-permute-done.1
  778.2 29.7 %fusion.4 = f32[1024,256]{1,0:T(8,128)S(1)} fusion(bf16[256,32768]{1,0:T(8,128)(2,1)} %copy-done, bf16[1,1024,32768]{2,1,0:T(8,128)(2,1)} %param.3), kind=kOutput, calls=%fused_computation.5 | convolution fusion | flops 17179869184 | bytes 84934656 | tf_op jit(solution)/shard_map/dot_general | solution.py:39
  807.9 0.9 constant_dynamic-slice_fusion.5
  808.8 1.0 collective-permute-start.3
  809.8 29.7 %fusion.2 = f32[1024,256]{1,0:T(8,128)S(1)} fusion(bf16[256,32768]{1,0:T(8,128)(2,1)} %collective-permute-done.5, bf16[1,1024,32768]{2,1,0:T(8,128)(2,1)} %param.3), kind=kOutput, calls=%fused_computation.3 | convolution fusion | flops 17179869184 | bytes 84934656 | tf_op jit(solution)/shard_map/dot_general | solution.py:39
  839.5 0.8 constant_dynamic-slice_fusion.3
  840.3 1.0 collective-permute-start.6
  841.3 255.8 %collective-permute-done.8 = bf16[256,32768]{1,0:T(8,128)(2,1)} collective-permute-done((bf16[256,32768]{1,0:T(8,128)(2,1)}, bf16[256,32768]{1,0:T(8,128)(2,1)}, u32[]{:S(2)}, u32[]{:S(2)}) %collective-permute-start.8) | collective-permute-done | bytes 16777248 | tf_op jit(solution)/shard_map/ppermute | solution.py:16
  1097.1 29.7 %fusion = f32[1024,256]{1,0:T(8,128)S(1)} fusion(bf16[256,32768]{1,0:T(8,128)(2,1)} %collective-permute-done.8, bf16[1,1024,32768]{2,1,0:T(8,128)(2,1)} %param.3), kind=kOutput, calls=%fused_computation.1 | convolution fusion | flops 17179869184 | bytes 84934656 | tf_op jit(solution)/shard_map/dot_general | solution.py:39
  1126.8 1.1 collective-permute-start.9
  1127.9 1.1 dynamic-slice_add_fusion.2
  1129.2 1.1 dynamic-slice_add_fusion.1
  1130.9 7.3 collective-permute-done.9
  1138.5 1.4 collective-permute-done.10
  1140.0 0.6 gather_fusion
  1141.2 29.6 %psum.7 = f32[1024]{0:T(1024)S(1)} all-reduce(f32[1024]{0:T(1024)S(1)} %bitcast.35), channel_id=1, replica_groups=mesh['grp'=2,'doc'=16] {'doc'}, use_global_device_ids=true, to_apply=%region_1.2 | all-reduce | flops 1024 | bytes 8192 | tf_op jit(solution)/shard_map/psum | solution.py:49
  1171.1 1.3 copy.4
  (34 shorter events, 2.3 us)
Async XLA Ops:
  0.0 365.5 %collective-permute-start.2 = (bf16[256,32768]{1,0:T(8,128)(2,1)}, bf16[256,32768]{1,0:T(8,128)(2,1)S(1)}, u32[]{:S(2)}, u32[]{:S(2)}) collective-permute-start(bf16[256,32768]{1,0:T(8,128)(2,1)} %bitcast.36), channel_id=1, source_target_pairs={{0,4},{1,5},{2,6},{3,7},{4,8},{5,9},{6,10},{7,11},{8,12},{9,13},{1... | collective-permute-start | bytes 50331656 | tf_op jit(solution)/shard_map/ppermute | solution.py:16
  365.5 5.7 copy-start
  371.2 363.3 %collective-permute-start.5 = (bf16[256,32768]{1,0:T(8,128)(2,1)S(1)}, bf16[256,32768]{1,0:T(8,128)(2,1)}, u32[]{:S(2)}, u32[]{:S(2)}) collective-permute-start(bf16[256,32768]{1,0:T(8,128)(2,1)S(1)} %collective-permute-done.2), channel_id=1, source_target_pairs={{0,4},{1,5},{2,6},{3,7},{4,8},{5,9},{6,10},{7,11},{8,12},{9,13},{1... | collective-permute-start | bytes 50331656 | tf_op jit(solution)/shard_map/ppermute | solution.py:16
  734.5 362.6 %collective-permute-start.8 = (bf16[256,32768]{1,0:T(8,128)(2,1)}, bf16[256,32768]{1,0:T(8,128)(2,1)}, u32[]{:S(2)}, u32[]{:S(2)}) collective-permute-start(bf16[256,32768]{1,0:T(8,128)(2,1)} %collective-permute-done.5), channel_id=1, source_target_pairs={{0,4},{1,5},{2,6},{3,7},{4,8},{5,9},{6,10},{7,11},{8,12},{9,13},{1... | collective-permute-start | bytes 50331656 | tf_op jit(solution)/shard_map/ppermute | solution.py:16
  764.2 12.3 %collective-permute-start = (f32[512,256]{1,0:T(8,128)S(1)}, f32[512,256]{1,0:T(8,128)S(1)}, u32[]{:S(2)}, u32[]{:S(2)}) collective-permute-start(f32[512,256]{1,0:T(8,128)S(1)} %constant_dynamic-slice_fusion.7), channel_id=1, source_target_pairs={{0,2},{1,3},{2,0},{3,1},{4,6},{5,7},{6,4},{7,5},{8,10},{9,11},{10,... | collective-permute-start | bytes 1572872 | tf_op jit(solution)/shard_map/ppermute | solution.py:10
  776.6 1.6 collective-permute-start.1
  808.8 319.2 %collective-permute-start.3 = (f32[512,256]{1,0:T(8,128)}, f32[512,256]{1,0:T(8,128)}, u32[]{:S(2)}, u32[]{:S(2)}) collective-permute-start(f32[512,256]{1,0:T(8,128)} %constant_dynamic-slice_fusion.5), channel_id=1, source_target_pairs={{0,2},{1,3},{2,0},{3,1},{4,6},{5,7},{6,4},{7,5},{8,10},{9,11},{10,... | collective-permute-start | bytes 1572872 | tf_op jit(solution)/shard_map/ppermute | solution.py:10
  840.3 288.9 %collective-permute-start.6 = (f32[512,256]{1,0:T(8,128)}, f32[512,256]{1,0:T(8,128)}, u32[]{:S(2)}, u32[]{:S(2)}) collective-permute-start(f32[512,256]{1,0:T(8,128)} %constant_dynamic-slice_fusion.3), channel_id=1, source_target_pairs={{0,2},{1,3},{2,0},{3,1},{4,6},{5,7},{6,4},{7,5},{8,10},{9,11},{10,... | collective-permute-start | bytes 1572872 | tf_op jit(solution)/shard_map/ppermute | solution.py:10
  1126.8 11.3 collective-permute-start.9
  1129.1 9.3 collective-permute-start.4
  1130.3 8.1 collective-permute-start.7
  1138.3 1.6 collective-permute-start.10
where the time goes:
time: 1170 us
  waiting for transfers between devices  1000 us (85%)
  matrix products  119 us (10%)
  blocking collectives  29.6 us (3%)
    ppermute x3, waiting for transfers between devices, shifted(): return lax.ppermute(value, axis, pairs)  982 us
    dot_general x4, matrix products, partial_scores(): lax.dot_general(query_tile, tile, contract, preferred_element_type=jnp.fl...  119 us
    psum x1, blocking collectives, on_device(): squares = lax.psum(jnp.sum(scores * scores, axis=0), 'doc')  29.6 us
  transfers between devices with their start and end apart: 11, of which 7 were waited for; matrix products, arithmetic and copies ran while one was open for 11% of the time, Pallas kernels for 0%

commit v1 on v0

v1 whole, which is shorter than its diff:
```python
import functools

import jax
import jax.numpy as jnp
from jax import lax
from jax.experimental import pallas as pl
from jax.experimental.pallas import tpu as pltpu
from jax.sharding import PartitionSpec as P

epsilon = 1e-06
groups = 4
chunks = 32
lent = 8
lag = 4
contract = (((1,), (1,)), ((), ()))


def link_phases(parts):
    kept = chunks - lent
    after = lent + parts * lent
    relay = max(after + lag, chunks + lent)
    final = max(relay + lag, 2 * kept)
    table = (
        ((0, lent, False, 0, 0), (lent, parts * lent, True, 0, 0), (after, kept, False, 0, lent)),
        ((0, kept, False, 0, lent), (kept, lent, False, 0, 0), (chunks, lent, False, 1, 0), (relay, kept, False, 1, lent)),
        ((0, kept, False, 0, lent), (kept, kept, False, 1, lent), (final, kept, False, 2, lent)),
    )
    ends = (
        (after + kept - 1,),
        (chunks - 1, relay + kept - 1),
        (kept - 1, 2 * kept - 1, final + kept - 1),
    )
    return table, ends, final + kept, after


def kernel(axis, dims, q_ref, d_ref, out_ref, held, lent_q, qbuf, dbuf, acc, lent_acc, red, lent_red, lent_sum, returned,
           squares, others, load_sem, send_sem, recv_sem, red_send, red_recv, lred_send, lred_recv, ret_send, ret_recv,
           sq_send, sq_recv):
    n, span, rows, docs, cols = dims
    parts = rows // docs
    width = cols // chunks
    share = rows // span
    table, ends, steps, lent_ready = link_phases(parts)
    me = lax.axis_index(axis)
    z = me // span
    b = me - z * span

    def at(index):
        return {axis: index}

    barrier = pltpu.get_barrier_semaphore()

    def greet(o, carry):
        pl.semaphore_signal(barrier, inc=1, device_id=at(lax.rem(me + o, n)), device_id_type=pl.DeviceIdType.MESH)
        return carry

    lax.fori_loop(1, n, greet, 0)
    pl.semaphore_wait(barrier, n - 1)

    def columns(chunk):
        return pl.ds(pl.multiple_of(chunk * width, width), width)

    def item(direction, sender, step):
        place = sender if direction == 0 else groups - 1 - sender
        is_doc = jnp.int32(0)
        is_query = jnp.int32(0)
        back = jnp.int32(0)
        chunk = jnp.int32(0)
        piece = jnp.int32(0)
        last = jnp.int32(0)
        for link, phases in enumerate(table):
            for first, count, query, behind, start in phases:
                hit = ((place == link) & (step >= first) & (step < first + count)).astype(jnp.int32)
                offset = step - first
                if query:
                    is_query = is_query + hit
                    chunk = chunk + hit * (start + offset // parts)
                    piece = piece + hit * (offset % parts)
                else:
                    is_doc = is_doc + hit
                    chunk = chunk + hit * (start + offset)
                    back = back + hit * behind
            for end in ends[link]:
                last = last + ((place == link) & (step == end)).astype(jnp.int32)
        block = sender - back if direction == 0 else sender + back
        return is_doc == 1, is_query == 1, block, chunk, piece, last == 1

    def target(direction):
        return lax.rem(me + (span if direction == 0 else n - span), n)

    def remote(direction, step, source, place):
        return pltpu.make_async_remote_copy(
            src_ref=source,
            dst_ref=place,
            send_sem=send_sem.at[direction, lax.rem(step, lag)],
            recv_sem=recv_sem.at[direction, step],
            device_id=at(target(direction)),
            device_id_type=pl.DeviceIdType.MESH,
        )

    def send(direction, step):
        is_doc, is_query, block, chunk, piece, _ = item(direction, z, step)

        @pl.when(is_doc & (block == z))
        def _():
            remote(direction, step, d_ref.at[:, columns(chunk)], held.at[z, :, columns(chunk)]).start()

        @pl.when(is_doc & (block != z))
        def _():
            remote(direction, step, held.at[block, :, columns(chunk)], held.at[block, :, columns(chunk)]).start()

        @pl.when(is_query)
        def _():
            taken = pl.ds(pl.multiple_of(piece * docs, docs), docs)
            remote(direction, step, q_ref.at[taken, columns(chunk)], lent_q.at[taken, columns(chunk)]).start()

    def wait_sent(direction, step):
        is_doc, is_query, _, _, _, _ = item(direction, z, step)

        @pl.when(is_doc | is_query)
        def _():
            remote(direction, step, d_ref.at[:, columns(0)], held.at[z, :, columns(0)]).wait_send()

    def wait_arrived(direction, step, arriving):
        is_doc, is_query, block, chunk, piece, _ = arriving

        @pl.when(is_doc)
        def _():
            place = held.at[block, :, columns(chunk)]
            remote(direction, step, place, place).wait_recv()

        @pl.when(is_query)
        def _():
            place = lent_q.at[pl.ds(pl.multiple_of(piece * docs, docs), docs), columns(chunk)]
            remote(direction, step, place, place).wait_recv()

    def load_queries(source, chunk, slot):
        return pltpu.make_async_copy(source.at[:, columns(chunk)], qbuf.at[slot], load_sem.at[0, slot])

    def load_documents(block, chunk, slot, start):
        own = pltpu.make_async_copy(d_ref.at[:, columns(chunk)], dbuf.at[slot], load_sem.at[1, slot])
        if not start:
            own.wait()
            return

        @pl.when(block == z)
        def _():
            own.start()

        @pl.when(block != z)
        def _():
            pltpu.make_async_copy(held.at[block, :, columns(chunk)], dbuf.at[slot], load_sem.at[1, slot]).start()

    def reduce_copy(block, o):
        peer = lax.rem(b + o, span)
        return pltpu.make_async_remote_copy(
            src_ref=acc.at[block, pl.ds(pl.multiple_of(peer * share, share), share), :],
            dst_ref=red.at[block, o - 1],
            send_sem=red_send.at[block],
            recv_sem=red_recv.at[block],
            device_id=at(z * span + peer),
            device_id_type=pl.DeviceIdType.MESH,
        )

    def reduce_send(block):
        def one(o, carry):
            reduce_copy(block, o).start()
            return carry

        lax.fori_loop(1, span, one, 0)

    own_rows = pl.ds(pl.multiple_of(b * share, share), share)
    middle = (z == 1) | (z == 2)
    first_lent = jnp.where(z <= 1, 1, 0)
    outward = jnp.where((z == 1) | (z == groups - 1), me - span, me + span)

    def lent_copy(o):
        peer = lax.rem(b + o, span)
        return pltpu.make_async_remote_copy(
            src_ref=lent_acc.at[:, pl.ds(pl.multiple_of(peer * share, share), share), :],
            dst_ref=lent_red.at[o - 1],
            send_sem=lred_send,
            recv_sem=lred_recv,
            device_id=at(z * span + peer),
            device_id_type=pl.DeviceIdType.MESH,
        )

    def return_copy():
        return pltpu.make_async_remote_copy(
            src_ref=lent_sum,
            dst_ref=returned,
            send_sem=ret_send,
            recv_sem=ret_recv,
            device_id=at(outward),
            device_id_type=pl.DeviceIdType.MESH,
        )

    acc[...] = jnp.zeros_like(acc)
    lent_acc[...] = jnp.zeros_like(lent_acc)
    squares[...] = jnp.zeros_like(squares)
    lent_step = lent_ready + lag
    lent_send = lent_step + lent
    lent_back = lent_send + 4

    def step_body(t, carry):
        before = t - lag
        rightward = item(0, z - 1, before)
        leftward = item(1, z + 1, before)
        wait_arrived(0, before, rightward)
        wait_arrived(1, before, leftward)
        for direction in (0, 1):
            wait_sent(direction, before)
            send(direction, t)

        jobs = (
            (rightward[0], rightward[2], rightward[3], rightward[5]),
            (leftward[0], leftward[2], leftward[3], leftward[5]),
            (t < chunks, z, t, t == chunks - 1),
        )
        for slot, (valid, block, chunk, _) in enumerate(jobs):

            @pl.when(valid)
            def _(slot=slot, block=block, chunk=chunk):
                load_queries(q_ref, chunk, slot).start()
                load_documents(block, chunk, slot, True)

        def multiply(slot, carry):
            def pick(which):
                values = [job[which].astype(jnp.int32) for job in jobs]
                return jnp.where(slot == 0, values[0], jnp.where(slot == 1, values[1], values[2]))

            block = pick(1)

            @pl.when(pick(0) == 1)
            def _():
                load_queries(q_ref, 0, slot).wait()
                load_documents(block, 0, slot, False)
                acc[block] += lax.dot_general(qbuf[slot], dbuf[slot], contract, preferred_element_type=jnp.float32)

                @pl.when(pick(3) == 1)
                def _():
                    reduce_send(block)

            return carry

        lax.fori_loop(0, 3, multiply, 0)

        @pl.when(middle & (t >= lent_step) & (t < lent_send))
        def _():
            chunk = t - lent_step
            load_queries(lent_q, chunk, 0).start()
            for j in range(groups - 1):
                load_documents(first_lent + j, chunk, j, True)
            load_queries(lent_q, chunk, 0).wait()

            def one(j, carry):
                load_documents(0, 0, j, False)
                lent_acc[j] += lax.dot_general(qbuf[0], dbuf[j], contract, preferred_element_type=jnp.float32)
                return carry

            lax.fori_loop(0, groups - 1, one, 0)

        @pl.when(middle & (t == lent_send))
        def _():
            def one(o, carry):
                lent_copy(o).start()
                return carry

            lax.fori_loop(1, span, one, 0)

        @pl.when(middle & (t == lent_back))
        def _():
            pltpu.make_async_copy(lent_red, lent_red, lred_recv).wait()
            lent_sum[...] = lent_acc[:, own_rows, :]

            def one(o, carry):
                lent_sum[...] += lent_red[o]
                return carry

            lax.fori_loop(0, span - 1, one, 0)
            return_copy().start()

        return carry

    lax.fori_loop(0, steps + lag, step_body, 0)

    for block in range(groups):
        here = pl.ds(block * docs, docs)
        pltpu.make_async_copy(red.at[block], red.at[block], red_recv.at[block]).wait()
        out_ref[:, here] = acc[block, own_rows, :]

        def one(o, carry):
            out_ref[:, here] += red[block, o]
            return carry

        lax.fori_loop(0, span - 1, one, 0)

    for edge, first in ((0, 1), (groups - 1, 0)):

        @pl.when(z == edge)
        def _(first=first):
            return_copy().wait_recv()
            for j in range(groups - 1):
                out_ref[:, pl.ds((first + j) * docs, docs)] += returned[j]

    for block in range(groups):
        value = out_ref[:, pl.ds(block * docs, docs)]
        squares[pl.ds(block, 1), :] = jnp.sum(value * value, axis=0, keepdims=True)

    def square_copy(o):
        return pltpu.make_async_remote_copy(
            src_ref=squares,
            dst_ref=others.at[o - 1],
            send_sem=sq_send,
            recv_sem=sq_recv,
            device_id=at(lax.rem(me + o, n)),
            device_id_type=pl.DeviceIdType.MESH,
        )

    def tell(o, carry):
        square_copy(o).start()
        return carry

    lax.fori_loop(1, n, tell, 0)
    pltpu.make_async_copy(others, others, sq_recv).wait()
    total = lax.fori_loop(0, n - 1, lambda o, value: value + others[o], squares[...])
    scale = lax.rsqrt(total / (groups * rows) + epsilon)
    for block in range(groups):
        here = pl.ds(block * docs, docs)
        out_ref[:, here] = out_ref[:, here] * scale[block:block + 1, :]

    pltpu.make_async_copy(others, others, sq_send).wait()
    for block in range(groups):
        pltpu.make_async_copy(red.at[block], red.at[block], red_send.at[block]).wait()

    @pl.when(middle)
    def _():
        pltpu.make_async_copy(lent_red, lent_red, lred_send).wait()
        return_copy().wait_send()


def on_device(doc_grads, query_grads):
    doc_tile = doc_grads[0]
    query_tile = query_grads[0]
    n = lax.axis_size("doc")
    span = n // groups
    docs, cols = doc_tile.shape
    rows = query_tile.shape[0]
    width = cols // chunks
    share = rows // span
    any_space = pl.BlockSpec(memory_space=pl.ANY)
    f32, bf16 = jnp.float32, jnp.bfloat16
    dma = pltpu.SemaphoreType.DMA
    steps = link_phases(rows // docs)[2]
    out, _, _ = pl.pallas_call(
        functools.partial(kernel, "doc", (n, span, rows, docs, cols)),
        out_shape=(
            jax.ShapeDtypeStruct((share, groups * docs), f32),
            jax.ShapeDtypeStruct((groups, docs, cols), bf16),
            jax.ShapeDtypeStruct((rows, lent * width), bf16),
        ),
        in_specs=[any_space, any_space],
        out_specs=(pl.BlockSpec(memory_space=pltpu.VMEM), any_space, any_space),
        scratch_shapes=[
            pltpu.VMEM((3, rows, width), bf16),
            pltpu.VMEM((3, docs, width), bf16),
            pltpu.VMEM((groups, rows, docs), f32),
            pltpu.VMEM((groups - 1, rows, docs), f32),
            pltpu.VMEM((groups, span - 1, share, docs), f32),
            pltpu.VMEM((span - 1, groups - 1, share, docs), f32),
            pltpu.VMEM((groups - 1, share, docs), f32),
            pltpu.VMEM((groups - 1, share, docs), f32),
            pltpu.VMEM((8, docs), f32),
            pltpu.VMEM((n - 1, 8, docs), f32),
            dma((2, 3)),
            dma((2, lag)),
            dma((2, steps)),
            dma((groups,)),
            dma((groups,)),
            dma,
            dma,
            dma,
            dma,
            dma,
            dma,
        ],
        compiler_params=pltpu.CompilerParams(
            collective_id=0, has_side_effects=True, vmem_limit_bytes=48 * 1024 * 1024
        ),
    )(query_tile, doc_tile)
    return out


def solution(mesh):
    placed = (P("doc", "grp", None), P("doc", "grp", None))
    return jax.shard_map(
        on_device, mesh=mesh, in_specs=placed, out_specs=P(("grp", "doc"), None), check_vma=False
    )
```

time: 1170 us -> 858 us (0.73)
  waiting for transfers between devices: 1000 us -> 0 us
  Pallas kernels: 0 us -> 855 us
  matrix products: 119 us -> 0 us
  blocking collectives: 29.6 us -> 0 us
    ppermute x11 -> x0, waiting for transfers between devices: 1000 us -> none  [the longest x3 982 us: shifted(): return lax.ppermute(value, axis, pairs)]
    pallas_call x0 -> x1, Pallas kernels: none -> 855 us  [on_device(): pl.pallas_call(functools.partial(kernel, 'doc', (n, span, rows, docs, col...]
    dot_general x4 -> x0, matrix products: 119 us -> none  [partial_scores(): lax.dot_general(query_tile, tile, contract, preferred_element_type=jnp.fl...]
    psum x1 -> x0, blocking collectives: 29.6 us -> none  [on_device(): squares = lax.psum(jnp.sum(scores * scores, axis=0), 'doc')]
  transfers between devices with their start and end apart: 11 -> 0, of which waited for: 7 -> 0; matrix products, arithmetic and copies ran while one was open for 11% -> 0% of each run, Pallas kernels for 0% -> 0%
where the time goes in v1:
time: 858 us; the launch traced here: 856 us
  Pallas kernels  855 us (100%)
    pallas_call x1, Pallas kernels, on_device(): pl.pallas_call(functools.partial(kernel, 'doc', (n, span, rows, docs, col...  855 us

profile of v1, /device:TPU:0, one launch (start us, length us, event | category | flops | bytes accessed | tf_op | source)
XLA Modules:
  0.0 855.9 jit_solution(11631539980461038134)
XLA Ops:
  0.0 854.9 %shard_map.28 = (f32[256,1024]{1,0:T(8,128)S(1)}, bf16[4,256,32768]{2,1,0:T(8,128)(2,1)}, bf16[1024,8192]{1,0:T(8,128)(2,1)}) custom-call(bf16[1024,32768]{1,0:T(8,128)(2,1)} %bitcast.q_ref, bf16[256,32768]{1,0:T(8,128)(2,1)} %bitcast.2), custom_call_target="tpu_custom_call" | custom-call | tf_op jit(solution)/shard_map/pallas_call | solution.py:355
  854.9 1.0 copy.4

commit v2 on v1

--- a/solution.py
+++ b/solution.py
@@ -9,13 +9,18 @@
 
 epsilon = 1e-06
 groups = 4
-chunks = 32
-lent = 8
-lag = 4
+most_chunks = 64
+lent_share = 9 / 32
+lag = 2
 contract = (((1,), (1,)), ((), ()))
 
 
-def link_phases(parts):
+def cut(cols):
+    chunks = min(most_chunks, cols // 128)
+    return chunks, int(chunks * lent_share)
+
+
+def link_phases(parts, chunks, lent):
     kept = chunks - lent
     after = lent + parts * lent
     relay = max(after + lag, chunks + lent)
@@ -38,9 +43,11 @@
            sq_send, sq_recv):
     n, span, rows, docs, cols = dims
     parts = rows // docs
+    chunks, lent = cut(cols)
     width = cols // chunks
     share = rows // span
-    table, ends, steps, lent_ready = link_phases(parts)
+    table, ends, steps, lent_ready = link_phases(parts, chunks, lent)
+    lent_ready = max(lent_ready, chunks + lent)
     me = lax.axis_index(axis)
     z = me // span
     b = me - z * span
@@ -195,9 +202,6 @@
             device_id_type=pl.DeviceIdType.MESH,
         )
 
-    acc[...] = jnp.zeros_like(acc)
-    lent_acc[...] = jnp.zeros_like(lent_acc)
-    squares[...] = jnp.zeros_like(squares)
     lent_step = lent_ready + lag
     lent_send = lent_step + lent
     lent_back = lent_send + 4
@@ -212,6 +216,12 @@
             wait_sent(direction, before)
             send(direction, t)
 
+        @pl.when(t == 0)
+        def _():
+            acc[...] = jnp.zeros_like(acc)
+            lent_acc[...] = jnp.zeros_like(lent_acc)
+            squares[...] = jnp.zeros_like(squares)
+
         jobs = (
             (rightward[0], rightward[2], rightward[3], rightward[5]),
             (leftward[0], leftward[2], leftward[3], leftward[5]),
@@ -346,12 +356,13 @@
     span = n // groups
     docs, cols = doc_tile.shape
     rows = query_tile.shape[0]
+    chunks, lent = cut(cols)
     width = cols // chunks
     share = rows // span
     any_space = pl.BlockSpec(memory_space=pl.ANY)
     f32, bf16 = jnp.float32, jnp.bfloat16
     dma = pltpu.SemaphoreType.DMA
-    steps = link_phases(rows // docs)[2]
+    steps = link_phases(rows // docs, chunks, lent)[2]
     out, _, _ = pl.pallas_call(
         functools.partial(kernel, "doc", (n, span, rows, docs, cols)),
         out_shape=(

time: 858 us -> 828 us (0.965)
  Pallas kernels: 855 us -> 823 us
    pallas_call x1, Pallas kernels: 855 us -> 823 us  [on_device(): pl.pallas_call(functools.partial(kernel, 'doc', (n, span, rows, docs, col...]
where the time goes in v2:
time: 828 us; the launch traced here: 824 us
  Pallas kernels  823 us (99%)
    pallas_call x1, Pallas kernels, on_device(): pl.pallas_call(functools.partial(kernel, 'doc', (n, span, rows, docs, col...  823 us

profile of v2, /device:TPU:0, one launch (start us, length us, event | category | flops | bytes accessed | tf_op | source)
XLA Modules:
  0.0 824.2 jit_solution(15147364955290447966)
XLA Ops:
  0.0 823.2 %shard_map.28 = (f32[256,1024]{1,0:T(8,128)S(1)}, bf16[4,256,32768]{2,1,0:T(8,128)(2,1)}, bf16[1024,9216]{1,0:T(8,128)(2,1)}) custom-call(bf16[1024,32768]{1,0:T(8,128)(2,1)} %bitcast.q_ref, bf16[256,32768]{1,0:T(8,128)(2,1)} %bitcast.2), custom_call_target="tpu_custom_call" | custom-call | tf_op jit(solution)/shard_map/pallas_call | solution.py:366
  823.2 1.0 copy.4
